TPU v7x, 32 devices: a whole 2x2x4 slice. The times are simulated.
32 devices in a mesh: row: 4 (over x, core), col: 8 (over z, y).
Axes of the slice: x: 2, y: 2, z: 4, core: 2. Of those that a mesh axis runs over, the one named last changes fastest.
Arguments:
- row_records: bfloat16 [8, 1024, 384], P('row', 'col'), may hold values from -6 to 6
- row_valid: int32 [8, 1024], P('row', 'col'), may hold values 0 or 1
- col_records: bfloat16 [8, 512, 384], P('col', 'row'), may hold values from -6 to 6
- col_valid: int32 [8, 512], P('col', 'row'), may hold values 0 or 1
Outputs:
- correlation: float32 [65, 512, 1024], P(None, 'row', 'col')
All inputs are finite; a program needn't handle non-finite values. No bound on the sum of `row_valid` or of `col_valid` on one device may be relied on, other than what follows from the above.
Results may differ from a plain program's by a relative error of at most 0.0003.
Values may be sent and summed in bfloat16 or wider, within the bound.
A program may use at most 128 MiB of HBM per device.

v0:
```python
import jax
import jax.numpy as jnp
from jax import lax
from jax.sharding import PartitionSpec as P

LAG = 32
STEPS = 4


def spread(block, axis, owner):
    block = jnp.where(lax.axis_index(axis) == owner, block, jnp.zeros_like(block))
    return lax.psum(block, axis)


def from_behind(value, axis, steps):
    count = lax.axis_size(axis)
    pairs = [(source, (source + steps) % count) for source in range(count)]
    return lax.ppermute(value, axis, pairs)


def shards(row_records, row_valid, col_records, col_valid):
    per_block = col_records.shape[0]
    samples = row_records.shape[2]
    col_count = lax.axis_size("col")
    blocks_per_row = col_count // lax.axis_size("row")
    col_here = lax.axis_index("col")
    row_masked = row_records * row_valid[:, :, None].astype(jnp.bfloat16)
    row_flags = row_valid.astype(jnp.bfloat16)
    col_masked = col_records * col_valid[:, :, None].astype(jnp.bfloat16)
    col_flags = col_valid.astype(jnp.bfloat16)
    left_parts = []
    left_flags = []
    for step in range(STEPS):
        target = (col_here - step) % col_count
        owner = target // blocks_per_row
        begin = target % blocks_per_row * per_block
        record = lax.dynamic_slice_in_dim(row_masked, begin, per_block, 0)
        flagged = lax.dynamic_slice_in_dim(row_flags, begin, per_block, 0)
        record, flagged = (spread(record, "row", owner), spread(flagged, "row", owner))
        left_parts.append(record)
        left_flags.append(flagged)
    right_parts = [None] * STEPS
    right_flags = [None] * STEPS
    current_rec, current_flag = (col_masked, col_flags)
    for step in range(STEPS):
        right_parts[step] = current_rec
        right_flags[step] = current_flag
        if step + 1 < STEPS:
            current_rec, current_flag = from_behind((current_rec, current_flag), "col", 1)
    left_all = jnp.concatenate(left_parts, axis=0)
    left_flag_all = jnp.concatenate(left_flags, axis=0)
    right_all = jnp.concatenate(right_parts, axis=0)
    right_flag_all = jnp.concatenate(right_flags, axis=0)
    count = jnp.dot(right_flag_all.T, left_flag_all, preferred_element_type=jnp.float32)
    windows = left_all.shape[0]
    row_width = left_all.shape[1]
    col_width = right_all.shape[1]
    left_flat = left_all.transpose(1, 0, 2).reshape(row_width, windows * samples)
    padded = jnp.pad(right_all.transpose(1, 0, 2), ((0, 0), (0, 0), (LAG, LAG)))
    lag_count = 2 * LAG + 1
    results = []
    for first in range(0, lag_count, 16):
        width = min(16, lag_count - first)
        stacked = jnp.stack(
            [padded[:, :, first + offset : first + offset + samples] for offset in range(width)],
            axis=0,
        )
        stacked = stacked.reshape(width * col_width, windows * samples)
        product = lax.dot_general(
            stacked, left_flat, (((1,), (1,)), ((), ())), preferred_element_type=jnp.float32
        )
        results.append(product.reshape(width, col_width, row_width))
    raw = jnp.concatenate(results, axis=0)
    return raw / (jnp.sqrt(jnp.float32(samples)) * jnp.maximum(count, 1.0))


def solution(mesh):
    return jax.shard_map(
        shards,
        mesh=mesh,
        in_specs=(P("row", "col", None), P("row", "col"), P("col", "row", None), P("col", "row")),
        out_specs=P(None, "row", "col"),
        check_vma=False,
    )
```

profile of v0, /device:TPU:0, one launch (start us, length us, event | category | flops | bytes accessed | tf_op | source)
XLA Modules:
  0.0 89.8 jit_solution(15776382211166775313)
XLA Ops:
  6.5 0.7 fusion.154
  7.2 1.0 %broadcast_multiply_fusion.1 = bf16[1,128,384]{2,1,0:T(8,128)(2,1)S(1)} fusion(bf16[1,128,384]{2,1,0:T(8,128)(2,1)} %param.6, bf16[128]{0:T(256)(128)(2,1)S(1)} %get-tuple-element.33), kind=kLoop, calls=%fused_computation.220 | loop fusion | flops 49152 | bytes 196864 | tf_op jit(solution)/shard_map/mul | solution.py:29
  8.2 3.0 %collective-permute-start = (bf16[1,128,384]{2,1,0:T(8,128)(2,1)S(1)}, bf16[1,128,384]{2,1,0:T(8,128)(2,1)S(1)}, u32[]{:S(2)}, u32[]{:S(2)}) collective-permute-start(bf16[1,128,384]{2,1,0:T(8,128)(2,1)S(1)} %broadcast_multiply_fusion.1), channel_id=1, source_target_pairs={{0,1},{1,2},{2,3},{3,4},{4,5},{5,6},{6,7},{7,0},{8,9},{9,10},{10,1... | collective-permute-start | bytes 294920 | tf_op jit(solution)/shard_map/ppermute | solution.py:18
  11.2 1.5 %collective-permute-start.3 = (bf16[1,128]{1,0:T(2,128)(2,1)S(1)}, bf16[1,128]{1,0:T(2,128)(2,1)S(1)}, u32[]{:S(2)}, u32[]{:S(2)}) collective-permute-start(bf16[1,128]{1,0:T(2,128)(2,1)S(1)} %get-tuple-element.32), channel_id=1, source_target_pairs={{0,1},{1,2},{2,3},{3,4},{4,5},{5,6},{6,7},{7,0},{8,9},{9,10},{10,1... | collective-permute-start | bytes 776 | tf_op jit(solution)/shard_map/ppermute | solution.py:18
  12.7 0.7 convert_element_type.21
  13.4 1.0 %broadcast_multiply_fusion = bf16[2,128,384]{2,1,0:T(8,128)(2,1)S(1)} fusion(bf16[2,128,384]{2,1,0:T(8,128)(2,1)} %param.4, bf16[2,128]{1,0:T(2,128)(2,1)S(1)} %convert_element_type.21), kind=kLoop, calls=%fused_computation.218 | loop fusion | flops 98304 | bytes 393728 | tf_op jit(solution)/shard_map/mul | solution.py:27
  14.5 0.8 dynamic-slice_select_fusion
  15.2 2.2 %collective-permute-done.3 = bf16[1,128]{1,0:T(2,128)(2,1)S(1)} collective-permute-done((bf16[1,128]{1,0:T(2,128)(2,1)S(1)}, bf16[1,128]{1,0:T(2,128)(2,1)S(1)}, u32[]{:S(2)}, u32[]{:S(2)}) %collective-permute-start.3) | collective-permute-done | bytes 288 | tf_op jit(solution)/shard_map/ppermute | solution.py:18
  17.5 6.2 %collective-permute-done.4 = bf16[1,128]{1,0:T(2,128)(2,1)S(1)} collective-permute-done((bf16[1,128]{1,0:T(2,128)(2,1)S(1)}, bf16[1,128]{1,0:T(2,128)(2,1)S(1)}, u32[]{:S(2)}, u32[]{:S(2)}) %collective-permute-start.4) | collective-permute-done | bytes 288 | tf_op jit(solution)/shard_map/ppermute | solution.py:18
  23.7 5.8 %all-reduce.1 = (bf16[1,128]{1,0:T(2,128)(2,1)S(1)}, bf16[1,128]{1,0:T(2,128)(2,1)S(1)}, bf16[1,128]{1,0:T(2,128)(2,1)S(1)}, bf16[1,128]{1,0:T(2,128)(2,1)S(1)}) all-reduce(bf16[1,128]{1,0:T(2,128)(2,1)S(1)} %get-tuple-element.29, bf16[1,128]{1,0:T(2,128)(2,1)S(1)} %get-tuple-element.30, ...), channel_id=1, replica_groups=mesh['row'=4,'col'=8] {'row'}, use_global_device_ids=true, to_apply=%region_7.8 | all-reduce | flops 512 | bytes 2048 | tf_op jit(solution)/shard_map/psum | solution.py:12
  29.5 0.4 collective-permute-done.5
  30.2 18.3 %all-reduce.5.cloned.1.call-done = (bf16[1,128,384]{2,1,0:T(8,128)(2,1)}, bf16[1,128,384]{2,1,0:T(8,128)(2,1)}, bf16[1,128,384]{2,1,0:T(8,128)(2,1)}, bf16[1,128,384]{2,1,0:T(8,128)(2,1)}) async-done(((bf16[1,128,384]{2,1,0:T(8,128)(2,1)}, bf16[1,128,384]{2,1,0:T(8,128)(2,1)}, bf16[1,128,384]{2,1,0:T(8,128)(2,1)}, bf16[1,128,384]{2,1,0:T(8,128)(2,1)}), (bf16[1,128,384]{2,1,0:T(8,128)(2,1)}, ...) | async-done | bytes 393232 | tf_op jit(solution)/shard_map/psum | solution.py:12
  48.5 0.9 %constant_dynamic-update-slice_fusion.3 = bf16[4,128,384]{2,1,0:T(8,128)(2,1)S(1)} fusion(bf16[1,128,384]{2,1,0:T(8,128)(2,1)} %get-tuple-element.9), kind=kLoop, calls=%fused_computation.213 | loop fusion | bytes 196608
  49.5 0.9 %constant_dynamic-update-slice_fusion.2 = bf16[4,128,384]{2,1,0:T(8,128)(2,1)S(1)} fusion(bf16[4,128,384]{2,1,0:T(8,128)(2,1)S(1)} %constant_dynamic-update-slice_fusion.3, bf16[1,128,384]{2,1,0:T(8,128)(2,1)} %get-tuple-element.10), kind=kLoop, calls=%fused_computation.212 | loop fusion | bytes 196608
  50.4 0.9 %constant_dynamic-update-slice_fusion.1 = bf16[4,128,384]{2,1,0:T(8,128)(2,1)S(1)} fusion(bf16[4,128,384]{2,1,0:T(8,128)(2,1)S(1)} %constant_dynamic-update-slice_fusion.2, bf16[1,128,384]{2,1,0:T(8,128)(2,1)} %get-tuple-element.11), kind=kLoop, calls=%fused_computation.211 | loop fusion | bytes 196608
  51.3 1.5 %collective-permute-start.2 = (bf16[1,128,384]{2,1,0:T(8,128)(2,1)S(1)}, bf16[1,128,384]{2,1,0:T(8,128)(2,1)S(1)}, u32[]{:S(2)}, u32[]{:S(2)}) collective-permute-start(bf16[1,128,384]{2,1,0:T(8,128)(2,1)S(1)} %collective-permute-done.1), channel_id=1, source_target_pairs={{0,1},{1,2},{2,3},{3,4},{4,5},{5,6},{6,7},{7,0},{8,9},{9,10},{10,1... | collective-permute-start | bytes 294920 | tf_op jit(solution)/shard_map/ppermute | solution.py:18
  52.8 0.9 %constant_dynamic-update-slice_fusion = bf16[4,128,384]{2,1,0:T(8,128)(2,1)S(1)} fusion(bf16[4,128,384]{2,1,0:T(8,128)(2,1)S(1)} %constant_dynamic-update-slice_fusion.1, bf16[1,128,384]{2,1,0:T(8,128)(2,1)} %get-tuple-element.12), kind=kLoop, calls=%fused_computation.210 | loop fusion | bytes 196608 | tf_op jit(solution)/shard_map/concatenate | solution.py:50
  53.7 4.9 %collective-permute-done.2 = bf16[1,128,384]{2,1,0:T(8,128)(2,1)S(1)} collective-permute-done((bf16[1,128,384]{2,1,0:T(8,128)(2,1)S(1)}, bf16[1,128,384]{2,1,0:T(8,128)(2,1)S(1)}, u32[]{:S(2)}, u32[]{:S(2)}) %collective-permute-start.2) | collective-permute-done | bytes 98336 | tf_op jit(solution)/shard_map/ppermute | solution.py:18
  61.7 0.4 fusion.129
  62.1 0.6 fusion.131
  65.5 0.5 fusion.99
  66.0 0.2 fusion.43
  66.5 0.2 fusion.47
  66.8 0.2 fusion.49
  67.0 0.2 fusion.51
  67.3 0.2 fusion.53
  67.5 0.2 fusion.55
  67.8 0.2 fusion.57
  68.0 0.2 fusion.59
  68.3 0.2 fusion.61
  68.5 0.2 fusion.63
  68.8 0.2 fusion.65
  69.0 0.2 fusion.67
  69.3 0.4 fusion.69
  69.7 0.2 fusion.15
  69.9 0.2 fusion.17
  70.2 0.2 fusion.19
  70.4 0.2 fusion.21
  70.7 0.2 fusion.23
  70.9 0.2 fusion.25
  71.2 0.2 fusion.27
  71.4 0.2 fusion.29
  72.9 1.8 %fusion.3 = f32[65,128,128]{2,1,0:T(8,128)S(1)} fusion(bf16[16,128,4,384]{3,1,2,0:T(8,128)(2,1)S(1)} %fusion.37, bf16[4,128,384]{2,1,0:T(8,128)(2,1)S(1)} %constant_dynamic-update-slice_fusion), kind=kOutput, calls=%fused_computation.8 | convolution fusion | flops 805306368 | bytes 7733248 | tf_op jit(solution)/shard_map/dot_general | solution.py:69
  74.7 1.8 %fusion.2 = f32[65,128,128]{2,1,0:T(8,128)S(1)} fusion(f32[65,128,128]{2,1,0:T(8,128)S(1)} %fusion.3, bf16[16,128,4,384]{3,1,2,0:T(8,128)(2,1)S(1)} %get-tuple-element.22, bf16[4,128,384]{2,1,0:T(8,128)(2,1)S(1)} %constant_dynamic-update-slice_fusion), kind=kOutput, calls=%fused_computation.6 | convolution fusion | flops 805306368 | bytes 7733248 | tf_op jit(solution)/shard_map/dot_general | solution.py:69
  76.5 1.8 %fusion.1 = f32[65,128,128]{2,1,0:T(8,128)S(1)} fusion(f32[65,128,128]{2,1,0:T(8,128)S(1)} %fusion.2, bf16[16,128,4,384]{3,1,2,0:T(8,128)(2,1)S(1)} %get-tuple-element.19, bf16[4,128,384]{2,1,0:T(8,128)(2,1)S(1)} %constant_dynamic-update-slice_fusion), kind=kOutput, calls=%fused_computation.4 | convolution fusion | flops 805306368 | bytes 7733248 | tf_op jit(solution)/shard_map/dot_general | solution.py:69
  78.4 1.8 %fusion = f32[65,128,128]{2,1,0:T(8,128)S(1)} fusion(f32[65,128,128]{2,1,0:T(8,128)S(1)} %fusion.1, bf16[16,128,4,384]{3,1,2,0:T(8,128)(2,1)S(1)} %get-tuple-element.13, bf16[4,128,384]{2,1,0:T(8,128)(2,1)S(1)} %constant_dynamic-update-slice_fusion), kind=kOutput, calls=%fused_computation.2 | convolution fusion | flops 805306368 | bytes 7733248 | tf_op jit(solution)/shard_map/dot_general | solution.py:69
  80.2 0.3 fusion.5
  80.5 2.4 %broadcast_divide_fusion = f32[65,128,128]{2,1,0:T(8,128)} fusion(f32[65,128,128]{2,1,0:T(8,128)S(1)} %fusion.5, f32[128,128]{1,0:T(8,128)S(1)} %fusion.4), kind=kLoop, calls=%fused_computation | loop fusion | flops 1064960 | bytes 8585216 | tf_op jit(solution)/shard_map/div | solution.py:74
  (42 shorter events, 7.2 us)
Async XLA Ops:
  6.5 42.0 %all-reduce.5.cloned.1.call-start = ((), (), s32[]{:S(2)}) async-start(), calls=%async_computation | async-start | bytes 786432 | tf_op jit(solution)/shard_map/psum | solution.py:12
  8.2 22.0 %collective-permute-start = (bf16[1,128,384]{2,1,0:T(8,128)(2,1)S(1)}, bf16[1,128,384]{2,1,0:T(8,128)(2,1)S(1)}, u32[]{:S(2)}, u32[]{:S(2)}) collective-permute-start(bf16[1,128,384]{2,1,0:T(8,128)(2,1)S(1)} %broadcast_multiply_fusion.1), channel_id=1, source_target_pairs={{0,1},{1,2},{2,3},{3,4},{4,5},{5,6},{6,7},{7,0},{8,9},{9,10},{10,1... | collective-permute-start | bytes 294920 | tf_op jit(solution)/shard_map/ppermute | solution.py:18
  11.2 6.2 %collective-permute-start.3 = (bf16[1,128]{1,0:T(2,128)(2,1)S(1)}, bf16[1,128]{1,0:T(2,128)(2,1)S(1)}, u32[]{:S(2)}, u32[]{:S(2)}) collective-permute-start(bf16[1,128]{1,0:T(2,128)(2,1)S(1)} %get-tuple-element.32), channel_id=1, source_target_pairs={{0,1},{1,2},{2,3},{3,4},{4,5},{5,6},{6,7},{7,0},{8,9},{9,10},{10,1... | collective-permute-start | bytes 776 | tf_op jit(solution)/shard_map/ppermute | solution.py:18
  17.4 6.2 %collective-permute-start.4 = (bf16[1,128]{1,0:T(2,128)(2,1)S(1)}, bf16[1,128]{1,0:T(2,128)(2,1)S(1)}, u32[]{:S(2)}, u32[]{:S(2)}) collective-permute-start(bf16[1,128]{1,0:T(2,128)(2,1)S(1)} %collective-permute-done.3), channel_id=1, source_target_pairs={{0,1},{1,2},{2,3},{3,4},{4,5},{5,6},{6,7},{7,0},{8,9},{9,10},{10,1... | collective-permute-start | bytes 776 | tf_op jit(solution)/shard_map/ppermute | solution.py:18
  23.7 6.2 %collective-permute-start.5 = (bf16[1,128]{1,0:T(2,128)(2,1)S(1)}, bf16[1,128]{1,0:T(2,128)(2,1)S(1)}, u32[]{:S(2)}, u32[]{:S(2)}) collective-permute-start(bf16[1,128]{1,0:T(2,128)(2,1)S(1)} %collective-permute-done.4), channel_id=1, source_target_pairs={{0,1},{1,2},{2,3},{3,4},{4,5},{5,6},{6,7},{7,0},{8,9},{9,10},{10,1... | collective-permute-start | bytes 776 | tf_op jit(solution)/shard_map/ppermute | solution.py:18
  30.2 21.1 %collective-permute-start.1 = (bf16[1,128,384]{2,1,0:T(8,128)(2,1)S(1)}, bf16[1,128,384]{2,1,0:T(8,128)(2,1)S(1)}, u32[]{:S(2)}, u32[]{:S(2)}) collective-permute-start(bf16[1,128,384]{2,1,0:T(8,128)(2,1)S(1)} %collective-permute-done), channel_id=1, source_target_pairs={{0,1},{1,2},{2,3},{3,4},{4,5},{5,6},{6,7},{7,0},{8,9},{9,10},{10,1... | collective-permute-start | bytes 294920 | tf_op jit(solution)/shard_map/ppermute | solution.py:18
  51.3 7.4 %collective-permute-start.2 = (bf16[1,128,384]{2,1,0:T(8,128)(2,1)S(1)}, bf16[1,128,384]{2,1,0:T(8,128)(2,1)S(1)}, u32[]{:S(2)}, u32[]{:S(2)}) collective-permute-start(bf16[1,128,384]{2,1,0:T(8,128)(2,1)S(1)} %collective-permute-done.1), channel_id=1, source_target_pairs={{0,1},{1,2},{2,3},{3,4},{4,5},{5,6},{6,7},{7,0},{8,9},{9,10},{10,1... | collective-permute-start | bytes 294920 | tf_op jit(solution)/shard_map/ppermute | solution.py:18
Sparse Core Ops, SparseCore 0:
  15.4 33.1 all-reduce.4
where the time goes:
time: 90.1 us; the launch traced here: 89.8 us
  waiting for transfers between devices  32.1 us (36%)
  local copies, waits for them, and re-layouts  16.9 us (19%)
  between operations  14.1 us (16%)
  matrix products  7.81 us (9%)
  other arithmetic  6.99 us (8%)
  starting transfers between devices  6.13 us (7%)
  blocking collectives  5.83 us (6%)
    psum x1, waiting for transfers between devices, spread(): return lax.psum(block, axis)  18.3 us
    unnamed x54, local copies, waits for them, and re-layouts  14.2 us
    ppermute x6, waiting for transfers between devices, from_behind(): return lax.ppermute(value, axis, pairs)  13.7 us
    dot_general x5, matrix products, shards(): lax.dot_general(stacked, left_flat, (((1,), (1,)), ((), ())), preferred_e...  7.58 us
    ppermute x6, starting transfers between devices, from_behind(): return lax.ppermute(value, axis, pairs)  6.13 us
    psum x1, blocking collectives, spread(): return lax.psum(block, axis)  5.83 us
    div x1, other arithmetic, shards(): return raw / (jnp.sqrt(jnp.float32(samples)) * jnp.maximum(count, 1.0))  2.45 us
  transfers between devices with their start and end apart: 7, of which 5 were waited for; matrix products, arithmetic and copies ran while one was open for 7% of the time, Pallas kernels for 0%

commit v1 on v0

v1 whole, which is shorter than its diff:
```python
import functools

import jax
import jax.numpy as jnp
from jax import lax
from jax.experimental import pallas as pl
from jax.experimental.pallas import tpu as pltpu
from jax.sharding import PartitionSpec as P

LAG = 32
STEPS = 4
FINE = 8
MESH = pl.DeviceIdType.MESH


def gather_kernel(
    nrow, ncol, rr, rv, cr, cv, left, left_flag, right, right_flag, flag_r, flag_c,
    send_l, send_lf, recv_l, recv_lf, send_c, send_cf, recv_c, recv_cf, local,
):
    r = lax.axis_index("row")
    c = lax.axis_index("col")
    held = rr.shape[0]
    barrier = pltpu.get_barrier_semaphore()
    for d in range(1, nrow):
        pl.semaphore_signal(barrier, inc=1, device_id={"row": lax.rem(r + d, nrow)}, device_id_type=MESH)
    for d in range(1, STEPS):
        pl.semaphore_signal(barrier, inc=1, device_id={"col": lax.rem(c + ncol - d, ncol)}, device_id_type=MESH)
    for i in range(held):
        flag_r[i] = jnp.broadcast_to(rv[i : i + 1, :].astype(jnp.float32), (16, rv.shape[1])).astype(jnp.bfloat16)
    flag_c[0] = jnp.broadcast_to(cv[0:1, :].astype(jnp.float32), (16, cv.shape[1])).astype(jnp.bfloat16)
    pl.semaphore_wait(barrier, nrow - 1 + STEPS - 1)

    def left_copies(i, d):
        slot = lax.rem(c + ncol - (r * held + i), ncol)
        slot = jnp.minimum(slot, STEPS - 1)
        to = {"row": lax.rem(r + d, nrow)}
        return (
            pltpu.make_async_remote_copy(
                rr.at[i], left.at[slot], send_l.at[i, d - 1], recv_l.at[slot], device_id=to, device_id_type=MESH
            ),
            pltpu.make_async_remote_copy(
                flag_r.at[i], left_flag.at[slot], send_lf.at[i, d - 1], recv_lf.at[slot], device_id=to, device_id_type=MESH
            ),
        )

    def left_own(i):
        slot = lax.rem(c + ncol - (r * held + i), ncol)
        slot = jnp.minimum(slot, STEPS - 1)
        return (
            pltpu.make_async_copy(rr.at[i], left.at[slot], local.at[2 * i]),
            pltpu.make_async_copy(flag_r.at[i], left_flag.at[slot], local.at[2 * i + 1]),
        )

    def right_copies(d):
        to = {"col": lax.rem(c + d, ncol)}
        return (
            pltpu.make_async_remote_copy(
                cr.at[0], right.at[d], send_c.at[d - 1], recv_c.at[d], device_id=to, device_id_type=MESH
            ),
            pltpu.make_async_remote_copy(
                flag_c.at[0], right_flag.at[d], send_cf.at[d - 1], recv_cf.at[d], device_id=to, device_id_type=MESH
            ),
        )

    def used(i):
        return lax.rem(c + ncol - (r * held + i), ncol) < STEPS

    own_right = (
        pltpu.make_async_copy(cr.at[0], right.at[0], local.at[2 * held]),
        pltpu.make_async_copy(flag_c.at[0], right_flag.at[0], local.at[2 * held + 1]),
    )
    for d in range(STEPS - 1, 0, -1):
        for copy in right_copies(d):
            copy.start()
    for i in range(held):
        @pl.when(used(i))
        def _():
            for d in range(nrow - 1, 0, -1):
                for copy in left_copies(i, d):
                    copy.start()
            for copy in left_own(i):
                copy.start()
    for copy in own_right:
        copy.start()

    for copy in own_right:
        copy.wait()
    for i in range(held):
        @pl.when(used(i))
        def _():
            for copy in left_own(i):
                copy.wait()
            for d in range(1, nrow):
                for copy in left_copies(i, d):
                    copy.wait_send()
    for d in range(1, STEPS):
        for copy in right_copies(d):
            copy.wait()
    for s in range(STEPS):
        owner = lax.div(lax.rem(c + ncol - s, ncol), held)

        @pl.when(owner != r)
        def _():
            to = {"row": lax.rem(r + 1, nrow)}
            pltpu.make_async_remote_copy(
                rr.at[0], left.at[s], send_l.at[0, 0], recv_l.at[s], device_id=to, device_id_type=MESH
            ).wait_recv()
            pltpu.make_async_remote_copy(
                flag_r.at[0], left_flag.at[s], send_lf.at[0, 0], recv_lf.at[s], device_id=to, device_id_type=MESH
            ).wait_recv()


def correlate_kernel(left, left_flag, right, right_flag, out, padded, stacked, shifted, weights, scale, result, sem):
    samples = left.shape[2]
    rows = left.shape[1]
    cols = right.shape[1]
    coarse = 2 * LAG // FINE + 1
    main = STEPS * samples
    count = jnp.zeros((cols, rows), jnp.float32)
    for w in range(STEPS):
        across = jnp.broadcast_to(right_flag[w, 0:1, :].astype(jnp.float32), (cols, cols)).T
        row_flag = left_flag[w, 0:1, :].astype(jnp.float32)
        count = count + across * row_flag
        mask = across.astype(jnp.bfloat16)
        padded[:, 0:128] = jnp.zeros((cols, 128), jnp.bfloat16)
        padded[:, 128 + samples :] = jnp.zeros((cols, 128), jnp.bfloat16)
        for j in range(samples // 128):
            padded[:, 128 * (j + 1) : 128 * (j + 2)] = right[w, :, 128 * j : 128 * (j + 1)] * mask
        for h in range(coarse):
            begin = 128 + FINE * h - LAG
            stacked[h * cols : (h + 1) * cols, w * samples : (w + 1) * samples] = padded[:, begin : begin + samples]
            stacked[h * cols : (h + 1) * cols, main + w * FINE : main + (w + 1) * FINE] = padded[
                :, begin + samples : begin + samples + FINE
            ]
        shifted[0:FINE, :] = jnp.zeros((FINE, rows), jnp.float32)
        shifted[FINE + samples :, :] = jnp.zeros((FINE, rows), jnp.float32)
        for j in range(samples // 128):
            block = left[w, :, 128 * j : 128 * (j + 1)].astype(jnp.float32).T * row_flag
            shifted[FINE + 128 * j : FINE + 128 * (j + 1), :] = block
        for g in range(FINE):
            weights[w * samples : (w + 1) * samples, g * rows : (g + 1) * rows] = shifted[
                FINE - g : FINE - g + samples, :
            ].astype(jnp.bfloat16)
            weights[main + w * FINE : main + (w + 1) * FINE, g * rows : (g + 1) * rows] = shifted[
                FINE - g + samples : 2 * FINE - g + samples, :
            ].astype(jnp.bfloat16)
    scale[...] = 1.0 / (jnp.sqrt(jnp.float32(samples)) * jnp.maximum(count, 1.0))

    copies = []
    for p in range(FINE // 2):
        for h in range(coarse):
            single = h == coarse - 1
            if single and p > 0:
                continue
            width = rows if single else 2 * rows
            product = jnp.dot(
                stacked[h * cols : (h + 1) * cols, :],
                weights[:, 2 * p * rows : 2 * p * rows + width],
                preferred_element_type=jnp.float32,
            )
            for q in range(width // rows):
                lag = FINE * h + 2 * p + q
                result[lag] = product[:, q * rows : (q + 1) * rows] * scale[...]
                copy = pltpu.make_async_copy(result.at[lag], out.at[lag], sem.at[lag])
                copy.start()
                copies.append(copy)
    for copy in copies:
        copy.wait()


def shards(row_records, row_valid, col_records, col_valid):
    nrow = lax.axis_size("row")
    ncol = lax.axis_size("col")
    held, rows, samples = row_records.shape
    cols = col_records.shape[1]
    lags = 2 * LAG + 1
    coarse = 2 * LAG // FINE + 1
    any_space = pl.BlockSpec(memory_space=pl.ANY)
    vmem = pl.BlockSpec(memory_space=pltpu.VMEM)
    dma = pltpu.SemaphoreType.DMA
    gathered = pl.pallas_call(
        functools.partial(gather_kernel, nrow, ncol),
        out_shape=(
            jax.ShapeDtypeStruct((STEPS, rows, samples), jnp.bfloat16),
            jax.ShapeDtypeStruct((STEPS, 16, rows), jnp.bfloat16),
            jax.ShapeDtypeStruct((STEPS, cols, samples), jnp.bfloat16),
            jax.ShapeDtypeStruct((STEPS, 16, cols), jnp.bfloat16),
        ),
        in_specs=[any_space, vmem, any_space, vmem],
        out_specs=(any_space,) * 4,
        scratch_shapes=[
            pltpu.VMEM((held, 16, rows), jnp.bfloat16),
            pltpu.VMEM((1, 16, cols), jnp.bfloat16),
            dma((held, nrow - 1)),
            dma((held, nrow - 1)),
            dma((STEPS,)),
            dma((STEPS,)),
            dma((STEPS - 1,)),
            dma((STEPS - 1,)),
            dma((STEPS,)),
            dma((STEPS,)),
            dma((2 * held + 2,)),
        ],
        compiler_params=pltpu.CompilerParams(collective_id=0, has_side_effects=True),
        name="gather",
    )(row_records, row_valid, col_records, col_valid)
    depth = STEPS * (samples + FINE)
    return pl.pallas_call(
        correlate_kernel,
        out_shape=jax.ShapeDtypeStruct((lags, cols, rows), jnp.float32),
        in_specs=[vmem] * 4,
        out_specs=any_space,
        scratch_shapes=[
            pltpu.VMEM((cols, samples + 256), jnp.bfloat16),
            pltpu.VMEM((coarse * cols, depth), jnp.bfloat16),
            pltpu.VMEM((samples + 2 * FINE, rows), jnp.float32),
            pltpu.VMEM((depth, FINE * rows), jnp.bfloat16),
            pltpu.VMEM((cols, rows), jnp.float32),
            pltpu.VMEM((lags, cols, rows), jnp.float32),
            dma((lags,)),
        ],
        compiler_params=pltpu.CompilerParams(vmem_limit_bytes=40 * 1024 * 1024),
        name="correlate",
    )(*gathered)


def solution(mesh):
    return jax.shard_map(
        shards,
        mesh=mesh,
        in_specs=(P("row", "col", None), P("row", "col"), P("col", "row", None), P("col", "row")),
        out_specs=P(None, "row", "col"),
        check_vma=False,
    )
```

time: 90.1 us -> 28.4 us (0.32)
  waiting for transfers between devices: 32.1 us -> 0 us
  Pallas kernels: 0 us -> 24.6 us
  between operations: 14.1 us -> 0.02 us
  local copies, waits for them, and re-layouts: 16.9 us -> 3.42 us
  matrix products: 7.81 us -> 0 us
  other arithmetic: 6.99 us -> 0 us
  starting transfers between devices: 6.13 us -> 0 us
  blocking collectives: 5.83 us -> 0 us
    pallas_call x0 -> x2, Pallas kernels: none -> 24.6 us  [the longest x1 17.6 us: shards(): pl.pallas_call(functools.partial(gather_kernel, nrow, ncol), out_shape=(j...]
    psum x1 -> x0, waiting for transfers between devices: 18.3 us -> none  [spread(): return lax.psum(block, axis)]
    ppermute x6 -> x0, waiting for transfers between devices: 13.7 us -> none  [from_behind(): return lax.ppermute(value, axis, pairs)]
    unnamed x54 -> x8, local copies, waits for them, and re-layouts: 14.2 us -> 3.42 us
    dot_general x6 -> x0, matrix products: 7.81 us -> none  [the longest x5 7.58 us: shards(): lax.dot_general(stacked, left_flat, (((1,), (1,)), ((), ())), preferred_e...]
    ppermute x6 -> x0, starting transfers between devices: 6.13 us -> none  [from_behind(): return lax.ppermute(value, axis, pairs)]
    psum x1 -> x0, blocking collectives: 5.83 us -> none  [spread(): return lax.psum(block, axis)]
    div x1 -> x0, other arithmetic: 2.45 us -> none  [shards(): return raw / (jnp.sqrt(jnp.float32(samples)) * jnp.maximum(count, 1.0))]
  transfers between devices with their start and end apart: 7 -> 0, of which waited for: 5 -> 0; matrix products, arithmetic and copies ran while one was open for 7% -> 0% of each run, Pallas kernels for 0% -> 0%
where the time goes in v1:
time: 28.4 us; the launch traced here: 28 us
  Pallas kernels  24.6 us (87%)
  local copies, waits for them, and re-layouts  3.42 us (12%)
    pallas_call x1, Pallas kernels, shards(): pl.pallas_call(functools.partial(gather_kernel, nrow, ncol), out_shape=(j...  17.6 us
    pallas_call x1, Pallas kernels, shards(): pl.pallas_call(correlate_kernel, out_shape=jax.ShapeDtypeStruct((lags, co...  6.99 us
    unnamed x8, local copies, waits for them, and re-layouts  3.42 us

profile of v1, /device:TPU:0, one launch (start us, length us, event | category | flops | bytes accessed | tf_op | source)
XLA Modules:
  0.0 28.0 jit_solution(1162862342153392525)
XLA Ops:
  0.0 17.6 %gather.1 = (bf16[4,128,384]{2,1,0:T(8,128)(2,1)}, bf16[4,16,128]{2,1,0:T(8,128)(2,1)}, bf16[4,128,384]{2,1,0:T(8,128)(2,1)}, bf16[4,16,128]{2,1,0:T(8,128)(2,1)}) custom-call(bf16[2,128,384]{2,1,0:T(8,128)(2,1)} %rr.1, s32[2,128]{1,0:T(2,128)} %rv.1, bf16[1,128,384]{2,1,0:T(8,128)(2,1)} %cr.1, s32[1,128]{1,0:T(1,128)} %cv.1), custom_call_target="tpu_custom_call" | custom-call | tf_op jit(solution)/shard_map/gather/pallas_call | solution.py:181
  17.6 0.0 copy-start
  17.6 1.0 %copy-done = bf16[4,128,384]{2,1,0:T(8,128)(2,1)S(1)} copy-done((bf16[4,128,384]{2,1,0:T(8,128)(2,1)S(1)}, bf16[4,128,384]{2,1,0:T(8,128)(2,1)}, u32[]{:S(2)}) %copy-start) | copy-done | bytes 393240
  18.6 0.0 copy-start.1
  18.6 1.0 %copy-done.1 = bf16[4,128,384]{2,1,0:T(8,128)(2,1)S(1)} copy-done((bf16[4,128,384]{2,1,0:T(8,128)(2,1)S(1)}, bf16[4,128,384]{2,1,0:T(8,128)(2,1)}, u32[]{:S(2)}) %copy-start.1) | copy-done | bytes 393240
  19.6 0.0 copy-start.2
  19.6 0.7 %copy-done.2 = bf16[4,16,128]{2,1,0:T(8,128)(2,1)S(1)} copy-done((bf16[4,16,128]{2,1,0:T(8,128)(2,1)S(1)}, bf16[4,16,128]{2,1,0:T(8,128)(2,1)}, u32[]{:S(2)}) %copy-start.2) | copy-done | bytes 16408
  20.3 0.0 copy-start.3
  20.3 0.7 %copy-done.3 = bf16[4,16,128]{2,1,0:T(8,128)(2,1)S(1)} copy-done((bf16[4,16,128]{2,1,0:T(8,128)(2,1)S(1)}, bf16[4,16,128]{2,1,0:T(8,128)(2,1)}, u32[]{:S(2)}) %copy-start.3) | copy-done | bytes 16408
  21.1 7.0 %correlate.1 = f32[65,128,128]{2,1,0:T(8,128)} custom-call(bf16[4,128,384]{2,1,0:T(8,128)(2,1)S(1)} %copy-done, bf16[4,16,128]{2,1,0:T(8,128)(2,1)S(1)} %copy-done.2, bf16[4,128,384]{2,1,0:T(8,128)(2,1)S(1)} %copy-done.1, bf16[4,16,128]{2,1,0:T(8,128)(2,1)S(1)} %copy-done.3), custom_call_target="tpu_custom_call" | custom-call | tf_op jit(solution)/shard_map/correlate/pallas_call | solution.py:208
Async XLA Ops:
  17.6 1.0 %copy-start = (bf16[4,128,384]{2,1,0:T(8,128)(2,1)S(1)}, bf16[4,128,384]{2,1,0:T(8,128)(2,1)}, u32[]{:S(2)}) copy-start(bf16[4,128,384]{2,1,0:T(8,128)(2,1)} %get-tuple-element.9.left) | copy-start | bytes 1179652
  18.6 1.0 %copy-start.1 = (bf16[4,128,384]{2,1,0:T(8,128)(2,1)S(1)}, bf16[4,128,384]{2,1,0:T(8,128)(2,1)}, u32[]{:S(2)}) copy-start(bf16[4,128,384]{2,1,0:T(8,128)(2,1)} %get-tuple-element.11.right) | copy-start | bytes 1179652
  19.6 0.7 %copy-start.2 = (bf16[4,16,128]{2,1,0:T(8,128)(2,1)S(1)}, bf16[4,16,128]{2,1,0:T(8,128)(2,1)}, u32[]{:S(2)}) copy-start(bf16[4,16,128]{2,1,0:T(8,128)(2,1)} %get-tuple-element.10.left_flag) | copy-start | bytes 49156
  20.3 0.7 %copy-start.3 = (bf16[4,16,128]{2,1,0:T(8,128)(2,1)S(1)}, bf16[4,16,128]{2,1,0:T(8,128)(2,1)}, u32[]{:S(2)}) copy-start(bf16[4,16,128]{2,1,0:T(8,128)(2,1)} %get-tuple-element.12.right_flag) | copy-start | bytes 49156

commit v2 on v0

v2 whole, which is shorter than its diff:
```python
import functools

import jax
import jax.numpy as jnp
from jax import lax
from jax.experimental import pallas as pl
from jax.experimental.pallas import tpu as pltpu
from jax.sharding import PartitionSpec as P

LAG = 32
STEPS = 4
FINE = 8
FLAG_ROWS = 16
MESH = pl.DeviceIdType.MESH


def gather_kernel(
    nrow, ncol, rr, rv, cr, cv, stacked, weights, scale,
    rr_here, rv_here, cr_here, cv_here, send_left, send_right, left, right, padded, shifted,
    in_sem, send_l, recv_l, pass_l, send_c, recv_c,
):
    r = lax.axis_index("row")
    c = lax.axis_index("col")
    held, rows, samples = rr.shape
    cols = cr.shape[1]
    tiles = samples // 128
    main = STEPS * samples
    coarse = 2 * LAG // FINE + 1
    even = lax.rem(c, 2) == 0
    other_core = r + 1 - 2 * lax.rem(r, 2)

    loads = [
        pltpu.make_async_copy(source, here, in_sem.at[k])
        for k, (source, here) in enumerate(((rv, rv_here), (cv, cv_here), (cr, cr_here), (rr, rr_here)))
    ]
    for load in loads:
        load.start()
    barrier = pltpu.get_barrier_semaphore()
    for d in range(1, nrow):
        pl.semaphore_signal(barrier, inc=1, device_id={"row": lax.rem(r + d, nrow)}, device_id_type=MESH)
    for d in (1, ncol - 1, ncol - 2):
        pl.semaphore_signal(barrier, inc=1, device_id={"col": lax.rem(c + d, ncol)}, device_id_type=MESH)
    for load in loads:
        load.wait()

    flag = cv_here[0:1, :].astype(jnp.float32)
    mask = jnp.broadcast_to(flag, (cols, cols)).T.astype(jnp.bfloat16)
    for j in range(tiles):
        send_right[128 * j : 128 * (j + 1), :] = cr_here[0, :, 128 * j : 128 * (j + 1)] * mask
    send_right[samples:, :] = jnp.broadcast_to(flag, (FLAG_ROWS, cols)).astype(jnp.bfloat16)
    for i in range(held):
        flag = rv_here[i : i + 1, :].astype(jnp.float32)
        for j in range(tiles):
            block = rr_here[i, :, 128 * j : 128 * (j + 1)].astype(jnp.float32).T * flag
            send_left[i, 128 * j : 128 * (j + 1), :] = block.astype(jnp.bfloat16)
        send_left[i, samples:, :] = jnp.broadcast_to(flag, (FLAG_ROWS, rows)).astype(jnp.bfloat16)
    pl.semaphore_wait(barrier, nrow - 1 + 3)

    def right_copy(source, slot, which, step):
        return pltpu.make_async_remote_copy(
            source, right.at[slot - 1], send_c.at[which], recv_c.at[slot - 1],
            device_id={"col": lax.rem(c + ncol + step, ncol)}, device_id_type=MESH,
        )

    def left_copy(source, slot, sender, to):
        return pltpu.make_async_remote_copy(
            source, left.at[slot], sender, recv_l.at[slot], device_id={"row": to}, device_id_type=MESH
        )

    def slot_of(i):
        return lax.rem(c + ncol - (r * held + i), ncol)

    def own_copies(i):
        slot = jnp.minimum(slot_of(i), STEPS - 1)
        copies = []
        for d in range(1, nrow // 2):
            chip = lax.rem(lax.div(r, 2) + d, nrow // 2)
            copies.append(left_copy(send_left.at[i], slot, send_l.at[i, d], 2 * chip + i % 2))
        copies.append(left_copy(send_left.at[i], slot, send_l.at[i, 0], other_core))
        return copies

    two_on = right_copy(send_right, 2, 0, 2)
    own_on = right_copy(send_right, 1, 1, 1)
    pass_back = right_copy(right.at[1], 1, 1, -1)
    pass_on = right_copy(right.at[1], 3, 2, 1)
    two_on.start()

    @pl.when(even)
    def _():
        own_on.start()

    for i in range(held):
        @pl.when(slot_of(i) < STEPS)
        def _():
            for copy in own_copies(i):
                copy.start()
            left[jnp.minimum(slot_of(i), STEPS - 1)] = send_left[i]

    padded[:, 0:128] = jnp.zeros((cols, 128), jnp.bfloat16)
    padded[:, 128 + samples :] = jnp.zeros((cols, 128), jnp.bfloat16)
    shifted[0:FINE, :] = jnp.zeros((FINE, rows), jnp.float32)
    shifted[FINE + samples :, :] = jnp.zeros((FINE, rows), jnp.float32)

    def stack(w, source):
        for j in range(tiles):
            padded[:, 128 * (j + 1) : 128 * (j + 2)] = source[128 * j : 128 * (j + 1), :]
        for h in range(coarse):
            begin = 128 + FINE * h - LAG
            lines = slice(h * cols, (h + 1) * cols)
            stacked[lines, w * samples : (w + 1) * samples] = padded[:, begin : begin + samples]
            stacked[lines, main + w * FINE : main + (w + 1) * FINE] = padded[:, begin + samples : begin + samples + FINE]

    def weigh(w):
        shifted[FINE : FINE + samples, :] = left[w, 0:samples, :].astype(jnp.float32)
        for g in range(FINE):
            lanes = slice(g * rows, (g + 1) * rows)
            weights[w * samples : (w + 1) * samples, lanes] = shifted[FINE - g : FINE - g + samples, :].astype(jnp.bfloat16)
            weights[main + w * FINE : main + (w + 1) * FINE, lanes] = shifted[
                FINE - g + samples : 2 * FINE - g + samples, :
            ].astype(jnp.bfloat16)

    stack(0, send_right)

    two_on.wait_recv()
    pass_on.start()

    @pl.when(jnp.logical_not(even))
    def _():
        pass_back.start()

    def facts(s):
        window = lax.rem(c + ncol - s, ncol)
        owner = lax.div(window, held)
        passes = jnp.logical_and(
            lax.div(owner, 2) != lax.div(r, 2), lax.rem(lax.rem(window, held), 2) == lax.rem(r, 2)
        )
        return owner, passes

    def pass_copy(s):
        return left_copy(left.at[s], s, pass_l.at[s], other_core)

    for s in range(STEPS):
        owner, passes = facts(s)

        @pl.when(passes)
        def _():
            left_copy(send_left.at[0], s, pass_l.at[s], other_core).wait_recv()
            pass_copy(s).start()

    stack(2, right.at[1])
    for s in range(STEPS):
        owner, passes = facts(s)

        @pl.when(jnp.logical_and(owner != r, jnp.logical_not(passes)))
        def _():
            left_copy(send_left.at[0], s, pass_l.at[s], other_core).wait_recv()

        weigh(s)
    own_on.wait_recv()
    stack(1, right.at[0])
    pass_on.wait_recv()
    stack(3, right.at[2])
    count = jnp.zeros((cols, rows), jnp.float32)
    for s in range(STEPS):
        source = send_right if s == 0 else right.at[s - 1]
        col_flag = source[samples : samples + FLAG_ROWS, :].astype(jnp.float32)[0:1, :]
        row_flag = left[s, samples : samples + FLAG_ROWS, :].astype(jnp.float32)[0:1, :]
        count = count + jnp.broadcast_to(col_flag, (cols, cols)).T * row_flag
    scale[...] = 1.0 / (jnp.sqrt(jnp.float32(samples)) * jnp.maximum(count, 1.0))

    two_on.wait_send()
    own_on.wait_send()
    pass_on.wait_send()
    for i in range(held):
        @pl.when(slot_of(i) < STEPS)
        def _():
            for copy in own_copies(i):
                copy.wait_send()
    for s in range(STEPS):
        owner, passes = facts(s)

        @pl.when(passes)
        def _():
            pass_copy(s).wait_send()


def correlate_kernel(stacked, weights, scale, out, result, sem):
    cols, rows = scale.shape
    coarse = stacked.shape[0] // cols
    copies = []
    for p in range(FINE // 2):
        for h in range(coarse):
            single = h == coarse - 1
            if single and p > 0:
                continue
            width = rows if single else 2 * rows
            product = jnp.dot(
                stacked[h * cols : (h + 1) * cols, :],
                weights[:, 2 * p * rows : 2 * p * rows + width],
                preferred_element_type=jnp.float32,
            )
            for q in range(width // rows):
                lag = FINE * h + 2 * p + q
                result[lag] = product[:, q * rows : (q + 1) * rows] * scale[...]
                copy = pltpu.make_async_copy(result.at[lag], out.at[lag], sem.at[lag])
                copy.start()
                copies.append(copy)
    for copy in copies:
        copy.wait()


def shards(row_records, row_valid, col_records, col_valid):
    nrow = lax.axis_size("row")
    ncol = lax.axis_size("col")
    held, rows, samples = row_records.shape
    cols = col_records.shape[1]
    lags = 2 * LAG + 1
    coarse = 2 * LAG // FINE + 1
    depth = STEPS * (samples + FINE)
    any_space = pl.BlockSpec(memory_space=pl.ANY)
    vmem = pl.BlockSpec(memory_space=pltpu.VMEM)
    dma = pltpu.SemaphoreType.DMA
    operands = pl.pallas_call(
        functools.partial(gather_kernel, nrow, ncol),
        out_shape=(
            jax.ShapeDtypeStruct((coarse * cols, depth), jnp.bfloat16),
            jax.ShapeDtypeStruct((depth, FINE * rows), jnp.bfloat16),
            jax.ShapeDtypeStruct((cols, rows), jnp.float32),
        ),
        in_specs=[pl.BlockSpec(memory_space=pltpu.HBM)] * 4,
        out_specs=(vmem,) * 3,
        scratch_shapes=[
            pltpu.VMEM((held, rows, samples), jnp.bfloat16),
            pltpu.VMEM((held, rows), jnp.int32),
            pltpu.VMEM((1, cols, samples), jnp.bfloat16),
            pltpu.VMEM((1, cols), jnp.int32),
            pltpu.VMEM((held, samples + FLAG_ROWS, rows), jnp.bfloat16),
            pltpu.VMEM((samples + FLAG_ROWS, cols), jnp.bfloat16),
            pltpu.VMEM((STEPS, samples + FLAG_ROWS, rows), jnp.bfloat16),
            pltpu.VMEM((STEPS - 1, samples + FLAG_ROWS, cols), jnp.bfloat16),
            pltpu.VMEM((cols, samples + 256), jnp.bfloat16),
            pltpu.VMEM((samples + 2 * FINE, rows), jnp.float32),
            dma((4,)),
            dma((held, nrow // 2)),
            dma((STEPS,)),
            dma((STEPS,)),
            dma((STEPS - 1,)),
            dma((STEPS - 1,)),
        ],
        compiler_params=pltpu.CompilerParams(
            collective_id=0, has_side_effects=True, vmem_limit_bytes=14 * 1024 * 1024
        ),
        name="gather",
    )(row_records, row_valid, col_records, col_valid)
    return pl.pallas_call(
        correlate_kernel,
        out_shape=jax.ShapeDtypeStruct((lags, cols, rows), jnp.float32),
        in_specs=[vmem] * 3,
        out_specs=any_space,
        scratch_shapes=[pltpu.VMEM((lags, cols, rows), jnp.float32), dma((lags,))],
        compiler_params=pltpu.CompilerParams(vmem_limit_bytes=16 * 1024 * 1024),
        name="correlate",
    )(*operands)


def solution(mesh):
    return jax.shard_map(
        shards,
        mesh=mesh,
        in_specs=(P("row", "col", None), P("row", "col"), P("col", "row", None), P("col", "row")),
        out_specs=P(None, "row", "col"),
        check_vma=False,
    )
```

time: 90.1 us -> 26.3 us (0.29)
  waiting for transfers between devices: 32.1 us -> 0 us
  Pallas kernels: 0 us -> 23 us
  between operations: 14.1 us -> 0.01 us
  local copies, waits for them, and re-layouts: 16.9 us -> 3.15 us
  matrix products: 7.81 us -> 0 us
  other arithmetic: 6.99 us -> 0 us
  starting transfers between devices: 6.13 us -> 0 us
  blocking collectives: 5.83 us -> 0 us
    pallas_call x0 -> x2, Pallas kernels: none -> 23 us  [the longest x1 17.5 us: shards(): pl.pallas_call(functools.partial(gather_kernel, nrow, ncol), out_shape=(j...]
    psum x1 -> x0, waiting for transfers between devices: 18.3 us -> none  [spread(): return lax.psum(block, axis)]
    ppermute x6 -> x0, waiting for transfers between devices: 13.7 us -> none  [from_behind(): return lax.ppermute(value, axis, pairs)]
    unnamed x54 -> x8, local copies, waits for them, and re-layouts: 14.2 us -> 3.15 us
    dot_general x6 -> x0, matrix products: 7.81 us -> none  [the longest x5 7.58 us: shards(): lax.dot_general(stacked, left_flat, (((1,), (1,)), ((), ())), preferred_e...]
    ppermute x6 -> x0, starting transfers between devices: 6.13 us -> none  [from_behind(): return lax.ppermute(value, axis, pairs)]
    psum x1 -> x0, blocking collectives: 5.83 us -> none  [spread(): return lax.psum(block, axis)]
    div x1 -> x0, other arithmetic: 2.45 us -> none  [shards(): return raw / (jnp.sqrt(jnp.float32(samples)) * jnp.maximum(count, 1.0))]
  transfers between devices with their start and end apart: 7 -> 0, of which waited for: 5 -> 0; matrix products, arithmetic and copies ran while one was open for 7% -> 0% of each run, Pallas kernels for 0% -> 0%
where the time goes in v2:
time: 26.3 us; the launch traced here: 26.1 us
  Pallas kernels  23 us (87%)
  local copies, waits for them, and re-layouts  3.15 us (12%)
    pallas_call x1, Pallas kernels, shards(): pl.pallas_call(functools.partial(gather_kernel, nrow, ncol), out_shape=(j...  17.5 us
    pallas_call x1, Pallas kernels, shards(): pl.pallas_call(correlate_kernel, out_shape=jax.ShapeDtypeStruct((lags, co...  5.42 us
    unnamed x8, local copies, waits for them, and re-layouts  3.15 us

profile of v2, /device:TPU:0, one launch (start us, length us, event | category | flops | bytes accessed | tf_op | source)
XLA Modules:
  0.0 26.1 jit_solution(14293839927772976868)
XLA Ops:
  0.0 0.0 copy-start
  0.0 0.9 %copy-done = bf16[2,128,384]{2,1,0:T(8,128)(2,1)S(1)} copy-done((bf16[2,128,384]{2,1,0:T(8,128)(2,1)S(1)}, bf16[2,128,384]{2,1,0:T(8,128)(2,1)}, u32[]{:S(2)}) %copy-start) | copy-done | bytes 196632
  0.9 0.0 copy-start.1
  0.9 0.9 %copy-done.1 = bf16[1,128,384]{2,1,0:T(8,128)(2,1)S(1)} copy-done((bf16[1,128,384]{2,1,0:T(8,128)(2,1)S(1)}, bf16[1,128,384]{2,1,0:T(8,128)(2,1)}, u32[]{:S(2)}) %copy-start.1) | copy-done | bytes 98328
  1.8 0.0 copy-start.2
  1.8 0.7 %copy-done.2 = s32[2,128]{1,0:T(2,128)S(1)} copy-done((s32[2,128]{1,0:T(2,128)S(1)}, s32[2,128]{1,0:T(2,128)}, u32[]{:S(2)}) %copy-start.2) | copy-done | bytes 1048
  2.5 0.0 copy-start.3
  2.5 0.7 %copy-done.3 = s32[1,128]{1,0:T(1,128)S(1)} copy-done((s32[1,128]{1,0:T(1,128)S(1)}, s32[1,128]{1,0:T(1,128)}, u32[]{:S(2)}) %copy-start.3) | copy-done | bytes 536
  3.2 17.5 %gather.1 = (bf16[1152,1568]{1,0:T(8,128)(2,1)S(1)}, bf16[1568,1024]{1,0:T(8,128)(2,1)S(1)}, f32[128,128]{1,0:T(8,128)S(1)}) custom-call(bf16[2,128,384]{2,1,0:T(8,128)(2,1)S(1)} %copy-done, s32[2,128]{1,0:T(2,128)S(1)} %copy-done.2, bf16[1,128,384]{2,1,0:T(8,128)(2,1)S(1)} %copy-done.1, s32[1,128]{1,0:T(1,128)S(1)} %copy-done.3), custom_call_target="tpu_custom_call" | custom-call | tf_op jit(solution)/shard_map/gather/pallas_call | solution.py:223
  20.7 5.4 %correlate.1 = f32[65,128,128]{2,1,0:T(8,128)} custom-call(bf16[1152,1568]{1,0:T(8,128)(2,1)S(1)} %get-tuple-element.8.stacked, bf16[1568,1024]{1,0:T(8,128)(2,1)S(1)} %get-tuple-element.9.weights, f32[128,128]{1,0:T(8,128)S(1)} %get-tuple-element.10.scale), custom_call_target="tpu_custom_call" | custom-call | tf_op jit(solution)/shard_map/correlate/pallas_call | solution.py:255
Async XLA Ops:
  0.0 0.9 %copy-start = (bf16[2,128,384]{2,1,0:T(8,128)(2,1)S(1)}, bf16[2,128,384]{2,1,0:T(8,128)(2,1)}, u32[]{:S(2)}) copy-start(bf16[2,128,384]{2,1,0:T(8,128)(2,1)} %rr.1) | copy-start | bytes 589828
  0.9 0.9 %copy-start.1 = (bf16[1,128,384]{2,1,0:T(8,128)(2,1)S(1)}, bf16[1,128,384]{2,1,0:T(8,128)(2,1)}, u32[]{:S(2)}) copy-start(bf16[1,128,384]{2,1,0:T(8,128)(2,1)} %cr.1) | copy-start | bytes 294916
  1.8 0.7 %copy-start.2 = (s32[2,128]{1,0:T(2,128)S(1)}, s32[2,128]{1,0:T(2,128)}, u32[]{:S(2)}) copy-start(s32[2,128]{1,0:T(2,128)} %rv.1) | copy-start | bytes 3076
  2.5 0.7 %copy-start.3 = (s32[1,128]{1,0:T(1,128)S(1)}, s32[1,128]{1,0:T(1,128)}, u32[]{:S(2)}) copy-start(s32[1,128]{1,0:T(1,128)} %cv.1) | copy-start | bytes 1540

commit v3 on v2

--- a/solution.py
+++ b/solution.py
@@ -15,8 +15,8 @@
 
 
 def gather_kernel(
-    nrow, ncol, rr, rv, cr, cv, stacked, weights, scale,
-    rr_here, rv_here, cr_here, cv_here, send_left, send_right, left, right, padded, shifted,
+    nrow, ncol, rr, rv, cr, cv, stacked, weights, partial, scale,
+    stacked_a, weights_a,    rr_here, rv_here, cr_here, cv_here, send_left, send_right, left, right, padded, shifted,
     in_sem, send_l, recv_l, pass_l, send_c, recv_c,
 ):
     r = lax.axis_index("row")
@@ -24,9 +24,9 @@
     held, rows, samples = rr.shape
     cols = cr.shape[1]
     tiles = samples // 128
-    main = STEPS * samples
     coarse = 2 * LAG // FINE + 1
     even = lax.rem(c, 2) == 0
+    neighbour = ncol + 1 - 2 * lax.rem(c, 2)
     other_core = r + 1 - 2 * lax.rem(r, 2)
 
     loads = [
@@ -38,8 +38,13 @@
     barrier = pltpu.get_barrier_semaphore()
     for d in range(1, nrow):
         pl.semaphore_signal(barrier, inc=1, device_id={"row": lax.rem(r + d, nrow)}, device_id_type=MESH)
-    for d in (1, ncol - 1, ncol - 2):
+    for d in (ncol - 2, neighbour):
         pl.semaphore_signal(barrier, inc=1, device_id={"col": lax.rem(c + d, ncol)}, device_id_type=MESH)
+
+    @pl.when(even)
+    def _():
+        pl.semaphore_signal(barrier, inc=1, device_id={"col": lax.rem(c + ncol - 3, ncol)}, device_id_type=MESH)
+
     for load in loads:
         load.wait()
 
@@ -54,13 +59,18 @@
             block = rr_here[i, :, 128 * j : 128 * (j + 1)].astype(jnp.float32).T * flag
             send_left[i, 128 * j : 128 * (j + 1), :] = block.astype(jnp.bfloat16)
         send_left[i, samples:, :] = jnp.broadcast_to(flag, (FLAG_ROWS, rows)).astype(jnp.bfloat16)
-    pl.semaphore_wait(barrier, nrow - 1 + 3)
+    pl.semaphore_wait(barrier, nrow - 1 + 2 + lax.rem(c, 2))
+
+    pieces = [slice(128 * j, 128 * (j + 1)) for j in range(tiles - 1)] + [slice(128 * (tiles - 1), samples + FLAG_ROWS)]
 
     def right_copy(source, slot, which, step):
-        return pltpu.make_async_remote_copy(
-            source, right.at[slot - 1], send_c.at[which], recv_c.at[slot - 1],
-            device_id={"col": lax.rem(c + ncol + step, ncol)}, device_id_type=MESH,
-        )
+        return [
+            pltpu.make_async_remote_copy(
+                source.at[lines], right.at[slot - 1, lines], send_c.at[which, k], recv_c.at[slot - 1, k],
+                device_id={"col": lax.rem(c + ncol + step, ncol)}, device_id_type=MESH,
+            )
+            for k, lines in enumerate(pieces)
+        ]
 
     def left_copy(source, slot, sender, to):
         return pltpu.make_async_remote_copy(
@@ -83,11 +93,19 @@
     own_on = right_copy(send_right, 1, 1, 1)
     pass_back = right_copy(right.at[1], 1, 1, -1)
     pass_on = right_copy(right.at[1], 3, 2, 1)
-    two_on.start()
+    three_on = right_copy(send_right, 3, 2, 3)
+    for piece in two_on:
+        piece.start()
+
+    @pl.when(jnp.logical_not(even))
+    def _():
+        for piece in three_on:
+            piece.start()
 
     @pl.when(even)
     def _():
-        own_on.start()
+        for piece in own_on:
+            piece.start()
 
     for i in range(held):
         @pl.when(slot_of(i) < STEPS)
@@ -101,32 +119,25 @@
     shifted[0:FINE, :] = jnp.zeros((FINE, rows), jnp.float32)
     shifted[FINE + samples :, :] = jnp.zeros((FINE, rows), jnp.float32)
 
-    def stack(w, source):
+    def stack(p, source):
+        target, begin_at = (stacked_a, p * samples) if p < STEPS - 1 else (stacked, 0)
         for j in range(tiles):
             padded[:, 128 * (j + 1) : 128 * (j + 2)] = source[128 * j : 128 * (j + 1), :]
         for h in range(coarse):
             begin = 128 + FINE * h - LAG
             lines = slice(h * cols, (h + 1) * cols)
-            stacked[lines, w * samples : (w + 1) * samples] = padded[:, begin : begin + samples]
-            stacked[lines, main + w * FINE : main + (w + 1) * FINE] = padded[:, begin + samples : begin + samples + FINE]
-
-    def weigh(w):
-        shifted[FINE : FINE + samples, :] = left[w, 0:samples, :].astype(jnp.float32)
+            target[lines, begin_at : begin_at + samples] = padded[:, begin : begin + samples]
+            stacked[lines, samples + p * FINE : samples + (p + 1) * FINE] = padded[:, begin + samples : begin + samples + FINE]
+
+    def weigh(p, slot):
+        target, begin_at = (weights_a, p * samples) if p < STEPS - 1 else (weights, 0)
+        shifted[FINE : FINE + samples, :] = left[slot, 0:samples, :].astype(jnp.float32)
         for g in range(FINE):
             lanes = slice(g * rows, (g + 1) * rows)
-            weights[w * samples : (w + 1) * samples, lanes] = shifted[FINE - g : FINE - g + samples, :].astype(jnp.bfloat16)
-            weights[main + w * FINE : main + (w + 1) * FINE, lanes] = shifted[
+            target[begin_at : begin_at + samples, lanes] = shifted[FINE - g : FINE - g + samples, :].astype(jnp.bfloat16)
+            weights[samples + p * FINE : samples + (p + 1) * FINE, lanes] = shifted[
                 FINE - g + samples : 2 * FINE - g + samples, :
             ].astype(jnp.bfloat16)
-
-    stack(0, send_right)
-
-    two_on.wait_recv()
-    pass_on.start()
-
-    @pl.when(jnp.logical_not(even))
-    def _():
-        pass_back.start()
 
     def facts(s):
         window = lax.rem(c + ncol - s, ncol)
@@ -139,6 +150,47 @@
     def pass_copy(s):
         return left_copy(left.at[s], s, pass_l.at[s], other_core)
 
+    def left_wait(s):
+        owner, passes = facts(s)
+
+        @pl.when(jnp.logical_and(owner != r, jnp.logical_not(passes)))
+        def _():
+            left_copy(send_left.at[0], s, pass_l.at[0], other_core).wait_recv()
+
+    def right_wait(slot):
+        for piece in right_copy(send_right, slot, 0, 2):
+            piece.wait_recv()
+
+    def multiply(first, last, add):
+        for p in range(FINE // 2):
+            for h in range(coarse):
+                single = h == coarse - 1
+                if single and p > 0:
+                    continue
+                width = rows if single else 2 * rows
+                product = jnp.dot(
+                    stacked_a[h * cols : (h + 1) * cols, first:last],
+                    weights_a[first:last, 2 * p * rows : 2 * p * rows + width],
+                    preferred_element_type=jnp.float32,
+                )
+                for q in range(width // rows):
+                    lag = FINE * h + 2 * p + q
+                    term = product[:, q * rows : (q + 1) * rows]
+                    partial[lag] = partial[lag] + term if add else term
+
+    stack(0, send_right)
+
+    for k in range(tiles):
+        two_on[k].wait_recv()
+
+        @pl.when(even)
+        def _():
+            pass_on[k].start()
+
+        @pl.when(jnp.logical_not(even))
+        def _():
+            pass_back[k].start()
+
     for s in range(STEPS):
         owner, passes = facts(s)
 
@@ -147,19 +199,22 @@
             left_copy(send_left.at[0], s, pass_l.at[s], other_core).wait_recv()
             pass_copy(s).start()
 
-    stack(2, right.at[1])
-    for s in range(STEPS):
-        owner, passes = facts(s)
-
-        @pl.when(jnp.logical_and(owner != r, jnp.logical_not(passes)))
-        def _():
-            left_copy(send_left.at[0], s, pass_l.at[s], other_core).wait_recv()
-
-        weigh(s)
-    own_on.wait_recv()
-    stack(1, right.at[0])
-    pass_on.wait_recv()
-    stack(3, right.at[2])
+    stack(1, right.at[1])
+    for p, slot in ((0, 0), (1, 2)):
+        left_wait(slot)
+        weigh(p, slot)
+    multiply(0, 2 * samples, False)
+    third = 1 + 2 * lax.rem(c + 1, 2)
+    fourth = 4 - third
+    right_wait(third)
+    stack(2, right.at[third - 1])
+    left_wait(third)
+    weigh(2, third)
+    multiply(2 * samples, 3 * samples, True)
+    right_wait(fourth)
+    stack(3, right.at[fourth - 1])
+    left_wait(fourth)
+    weigh(3, fourth)
     count = jnp.zeros((cols, rows), jnp.float32)
     for s in range(STEPS):
         source = send_right if s == 0 else right.at[s - 1]
@@ -168,9 +223,8 @@
         count = count + jnp.broadcast_to(col_flag, (cols, cols)).T * row_flag
     scale[...] = 1.0 / (jnp.sqrt(jnp.float32(samples)) * jnp.maximum(count, 1.0))
 
-    two_on.wait_send()
-    own_on.wait_send()
-    pass_on.wait_send()
+    for piece in two_on + own_on + pass_on:
+        piece.wait_send()
     for i in range(held):
         @pl.when(slot_of(i) < STEPS)
         def _():
@@ -184,7 +238,7 @@
             pass_copy(s).wait_send()
 
 
-def correlate_kernel(stacked, weights, scale, out, result, sem):
+def correlate_kernel(stacked, weights, partial, scale, out, result, sem):
     cols, rows = scale.shape
     coarse = stacked.shape[0] // cols
     copies = []
@@ -201,7 +255,7 @@
             )
             for q in range(width // rows):
                 lag = FINE * h + 2 * p + q
-                result[lag] = product[:, q * rows : (q + 1) * rows] * scale[...]
+                result[lag] = (partial[lag] + product[:, q * rows : (q + 1) * rows]) * scale[...]
                 copy = pltpu.make_async_copy(result.at[lag], out.at[lag], sem.at[lag])
                 copy.start()
                 copies.append(copy)
@@ -216,20 +270,24 @@
     cols = col_records.shape[1]
     lags = 2 * LAG + 1
     coarse = 2 * LAG // FINE + 1
-    depth = STEPS * (samples + FINE)
+    early = (STEPS - 1) * samples
+    late = samples + STEPS * FINE
     any_space = pl.BlockSpec(memory_space=pl.ANY)
     vmem = pl.BlockSpec(memory_space=pltpu.VMEM)
     dma = pltpu.SemaphoreType.DMA
     operands = pl.pallas_call(
         functools.partial(gather_kernel, nrow, ncol),
         out_shape=(
-            jax.ShapeDtypeStruct((coarse * cols, depth), jnp.bfloat16),
-            jax.ShapeDtypeStruct((depth, FINE * rows), jnp.bfloat16),
+            jax.ShapeDtypeStruct((coarse * cols, late), jnp.bfloat16),
+            jax.ShapeDtypeStruct((late, FINE * rows), jnp.bfloat16),
+            jax.ShapeDtypeStruct((lags, cols, rows), jnp.float32),
             jax.ShapeDtypeStruct((cols, rows), jnp.float32),
         ),
         in_specs=[pl.BlockSpec(memory_space=pltpu.HBM)] * 4,
-        out_specs=(vmem,) * 3,
+        out_specs=(vmem,) * 4,
         scratch_shapes=[
+            pltpu.VMEM((coarse * cols, early), jnp.bfloat16),
+            pltpu.VMEM((early, FINE * rows), jnp.bfloat16),
             pltpu.VMEM((held, rows, samples), jnp.bfloat16),
             pltpu.VMEM((held, rows), jnp.int32),
             pltpu.VMEM((1, cols, samples), jnp.bfloat16),
@@ -244,18 +302,18 @@
             dma((held, nrow // 2)),
             dma((STEPS,)),
             dma((STEPS,)),
-            dma((STEPS - 1,)),
-            dma((STEPS - 1,)),
+            dma((STEPS - 1, samples // 128)),
+            dma((STEPS - 1, samples // 128)),
         ],
         compiler_params=pltpu.CompilerParams(
-            collective_id=0, has_side_effects=True, vmem_limit_bytes=14 * 1024 * 1024
+            collective_id=0, has_side_effects=True, vmem_limit_bytes=20 * 1024 * 1024
         ),
         name="gather",
-    )(row_records, row_valid, col_records, col_valid)
+    )(*(pltpu.with_memory_space_constraint(x, pltpu.HBM) for x in (row_records, row_valid, col_records, col_valid)))
     return pl.pallas_call(
         correlate_kernel,
         out_shape=jax.ShapeDtypeStruct((lags, cols, rows), jnp.float32),
-        in_specs=[vmem] * 3,
+        in_specs=[vmem] * 4,
         out_specs=any_space,
         scratch_shapes=[pltpu.VMEM((lags, cols, rows), jnp.float32), dma((lags,))],
         compiler_params=pltpu.CompilerParams(vmem_limit_bytes=16 * 1024 * 1024),

time: 26.3 us -> 20.1 us (0.76)
  local copies, waits for them, and re-layouts: 3.15 us -> 0 us
  Pallas kernels: 23 us -> 20 us
    unnamed x8 -> x0, local copies, waits for them, and re-layouts: 3.15 us -> none
    pallas_call x1, Pallas kernels: 5.42 us -> 2.8 us  [shards(): pl.pallas_call(correlate_kernel, out_shape=jax.ShapeDtypeStruct((lags, co...]
    pallas_call x1, Pallas kernels: 17.5 us -> 17.2 us  [shards(): pl.pallas_call(functools.partial(gather_kernel, nrow, ncol), out_shape=(j...]
where the time goes in v3:
time: 20.1 us; the launch traced here: 20 us
  Pallas kernels  20 us (100%)
    pallas_call x1, Pallas kernels, shards(): pl.pallas_call(functools.partial(gather_kernel, nrow, ncol), out_shape=(j...  17.2 us
    pallas_call x1, Pallas kernels, shards(): pl.pallas_call(correlate_kernel, out_shape=jax.ShapeDtypeStruct((lags, co...  2.8 us

profile of v3, /device:TPU:0, one launch (start us, length us, event | category | flops | bytes accessed | tf_op | source)
XLA Modules:
  0.0 20.0 jit_solution(912708515063254471)
XLA Ops:
  0.0 17.2 %gather.1 = (bf16[1152,416]{1,0:T(8,128)(2,1)S(1)}, bf16[416,1024]{1,0:T(8,128)(2,1)S(1)}, f32[65,128,128]{2,1,0:T(8,128)S(1)}, f32[128,128]{1,0:T(8,128)S(1)}) custom-call(bf16[2,128,384]{2,1,0:T(8,128)(2,1)} %rr.1, s32[2,128]{1,0:T(2,128)} %rv.1, bf16[1,128,384]{2,1,0:T(8,128)(2,1)} %cr.1, s32[1,128]{1,0:T(1,128)} %cv.1), custom_call_target="tpu_custom_call" | custom-call | tf_op jit(solution)/shard_map/gather/pallas_call | solution.py:278
  17.2 2.8 %correlate.1 = f32[65,128,128]{2,1,0:T(8,128)} custom-call(bf16[1152,416]{1,0:T(8,128)(2,1)S(1)} %get-tuple-element.9.stacked, bf16[416,1024]{1,0:T(8,128)(2,1)S(1)} %get-tuple-element.10.weights, f32[65,128,128]{2,1,0:T(8,128)S(1)} %get-tuple-element.11.partial, f32[128,128]{1,0:T(8,128)S(1)} %get-tuple-element.12.scale), custom_call_target="tpu_custom_call" | custom-call | tf_op jit(solution)/shard_map/correlate/pallas_call | solution.py:313

commit v4 on v3

--- a/solution.py
+++ b/solution.py
@@ -17,7 +17,7 @@
 def gather_kernel(
     nrow, ncol, rr, rv, cr, cv, stacked, weights, partial, scale,
     stacked_a, weights_a,    rr_here, rv_here, cr_here, cv_here, send_left, send_right, left, right, padded, shifted,
-    in_sem, send_l, recv_l, pass_l, send_c, recv_c,
+    in_sem, send_l, recv_l, pass_l, send_c, recv_c, send_relay, recv_relay, relay,
 ):
     r = lax.axis_index("row")
     c = lax.axis_index("col")
@@ -31,35 +31,25 @@
 
     loads = [
         pltpu.make_async_copy(source, here, in_sem.at[k])
-        for k, (source, here) in enumerate(((rv, rv_here), (cv, cv_here), (cr, cr_here), (rr, rr_here)))
+        for k, (source, here) in enumerate(((cv, cv_here), (cr, cr_here), (rv, rv_here), (rr, rr_here)))
     ]
     for load in loads:
         load.start()
     barrier = pltpu.get_barrier_semaphore()
     for d in range(1, nrow):
         pl.semaphore_signal(barrier, inc=1, device_id={"row": lax.rem(r + d, nrow)}, device_id_type=MESH)
-    for d in (ncol - 2, neighbour):
+    for d in (ncol - 2, ncol - 4, neighbour):
         pl.semaphore_signal(barrier, inc=1, device_id={"col": lax.rem(c + d, ncol)}, device_id_type=MESH)
 
-    @pl.when(even)
-    def _():
-        pl.semaphore_signal(barrier, inc=1, device_id={"col": lax.rem(c + ncol - 3, ncol)}, device_id_type=MESH)
-
-    for load in loads:
-        load.wait()
+    loads[0].wait()
+    loads[1].wait()
 
     flag = cv_here[0:1, :].astype(jnp.float32)
     mask = jnp.broadcast_to(flag, (cols, cols)).T.astype(jnp.bfloat16)
     for j in range(tiles):
         send_right[128 * j : 128 * (j + 1), :] = cr_here[0, :, 128 * j : 128 * (j + 1)] * mask
     send_right[samples:, :] = jnp.broadcast_to(flag, (FLAG_ROWS, cols)).astype(jnp.bfloat16)
-    for i in range(held):
-        flag = rv_here[i : i + 1, :].astype(jnp.float32)
-        for j in range(tiles):
-            block = rr_here[i, :, 128 * j : 128 * (j + 1)].astype(jnp.float32).T * flag
-            send_left[i, 128 * j : 128 * (j + 1), :] = block.astype(jnp.bfloat16)
-        send_left[i, samples:, :] = jnp.broadcast_to(flag, (FLAG_ROWS, rows)).astype(jnp.bfloat16)
-    pl.semaphore_wait(barrier, nrow - 1 + 2 + lax.rem(c, 2))
+    pl.semaphore_wait(barrier, nrow - 1 + 3)
 
     pieces = [slice(128 * j, 128 * (j + 1)) for j in range(tiles - 1)] + [slice(128 * (tiles - 1), samples + FLAG_ROWS)]
 
@@ -85,7 +75,7 @@
         copies = []
         for d in range(1, nrow // 2):
             chip = lax.rem(lax.div(r, 2) + d, nrow // 2)
-            copies.append(left_copy(send_left.at[i], slot, send_l.at[i, d], 2 * chip + i % 2))
+            copies.append(left_copy(send_left.at[i], slot, send_l.at[i, d], 2 * chip + lax.rem(i, 2)))
         copies.append(left_copy(send_left.at[i], slot, send_l.at[i, 0], other_core))
         return copies
 
@@ -93,21 +83,44 @@
     own_on = right_copy(send_right, 1, 1, 1)
     pass_back = right_copy(right.at[1], 1, 1, -1)
     pass_on = right_copy(right.at[1], 3, 2, 1)
-    three_on = right_copy(send_right, 3, 2, 3)
+
+    cut = FLAG_ROWS * -(-(samples + FLAG_ROWS) // (2 * FLAG_ROWS))
+    upper, lower, lower_here = slice(0, cut), slice(cut, samples + FLAG_ROWS), slice(0, samples + FLAG_ROWS - cut)
+
+    def relay_copy(source, target, sender, receiver, step):
+        return pltpu.make_async_remote_copy(
+            source, target, send_relay.at[sender], receiver,
+            device_id={"col": lax.rem(c + ncol + step, ncol)}, device_id_type=MESH,
+        )
+
+    upper_out = relay_copy(send_right.at[upper], relay.at[upper], 0, recv_relay.at[0], -1)
+    lower_out = relay_copy(send_right.at[lower], relay.at[lower_here], 1, recv_relay.at[0], 4)
+    upper_on = relay_copy(relay.at[upper], right.at[2, upper], 0, recv_c.at[2, 0], 4)
+    lower_on = relay_copy(relay.at[lower_here], right.at[2, lower], 2, recv_c.at[2, 1], -1)
     for piece in two_on:
         piece.start()
 
     @pl.when(jnp.logical_not(even))
     def _():
-        for piece in three_on:
-            piece.start()
+        upper_out.start()
+        lower_out.start()
 
     @pl.when(even)
     def _():
         for piece in own_on:
             piece.start()
 
+    loads[2].wait()
+    loads[3].wait()
     for i in range(held):
+        flag = rv_here[i : i + 1, :].astype(jnp.float32)
+        for j in range(tiles):
+            block = rr_here[i, :, 128 * j : 128 * (j + 1)].astype(jnp.float32).T * flag
+            send_left[i, 128 * j : 128 * (j + 1), :] = block.astype(jnp.bfloat16)
+        send_left[i, samples:, :] = jnp.broadcast_to(flag, (FLAG_ROWS, rows)).astype(jnp.bfloat16)
+    for k in range(held):
+        i = lax.rem(c + k, held)
+
         @pl.when(slot_of(i) < STEPS)
         def _():
             for copy in own_copies(i):
@@ -178,7 +191,24 @@
                     term = product[:, q * rows : (q + 1) * rows]
                     partial[lag] = partial[lag] + term if add else term
 
+    def left_pass(s):
+        owner, passes = facts(s)
+
+        @pl.when(passes)
+        def _():
+            left_copy(send_left.at[0], s, pass_l.at[s], other_core).wait_recv()
+            pass_copy(s).start()
+
+    @pl.when(even)
+    def _():
+        upper_out.wait_recv()
+        upper_on.start()
+
     stack(0, send_right)
+    left_pass(0)
+    left_wait(0)
+    weigh(0, 0)
+    multiply(0, samples, False)
 
     for k in range(tiles):
         two_on[k].wait_recv()
@@ -191,30 +221,34 @@
         def _():
             pass_back[k].start()
 
-    for s in range(STEPS):
-        owner, passes = facts(s)
-
-        @pl.when(passes)
-        def _():
-            left_copy(send_left.at[0], s, pass_l.at[s], other_core).wait_recv()
-            pass_copy(s).start()
-
+    @pl.when(jnp.logical_not(even))
+    def _():
+        lower_out.wait_recv()
+        lower_on.start()
+
+    for s in (2, 1, 3):
+        left_pass(s)
     stack(1, right.at[1])
-    for p, slot in ((0, 0), (1, 2)):
-        left_wait(slot)
-        weigh(p, slot)
-    multiply(0, 2 * samples, False)
-    third = 1 + 2 * lax.rem(c + 1, 2)
-    fourth = 4 - third
-    right_wait(third)
-    stack(2, right.at[third - 1])
-    left_wait(third)
-    weigh(2, third)
+    left_wait(2)
+    weigh(1, 2)
+    multiply(samples, 2 * samples, True)
+    left_wait(1)
+    weigh(2, 1)
+    right_wait(1)
+    stack(2, right.at[0])
     multiply(2 * samples, 3 * samples, True)
-    right_wait(fourth)
-    stack(3, right.at[fourth - 1])
-    left_wait(fourth)
-    weigh(3, fourth)
+    left_wait(3)
+    weigh(3, 3)
+    @pl.when(even)
+    def _():
+        upper_on.wait_recv()
+        lower_on.wait_recv()
+
+    @pl.when(jnp.logical_not(even))
+    def _():
+        right_wait(3)
+
+    stack(3, right.at[2])
     count = jnp.zeros((cols, rows), jnp.float32)
     for s in range(STEPS):
         source = send_right if s == 0 else right.at[s - 1]
@@ -223,8 +257,20 @@
         count = count + jnp.broadcast_to(col_flag, (cols, cols)).T * row_flag
     scale[...] = 1.0 / (jnp.sqrt(jnp.float32(samples)) * jnp.maximum(count, 1.0))
 
-    for piece in two_on + own_on + pass_on:
+    for piece in two_on + own_on:
         piece.wait_send()
+    upper_out.wait_send()
+
+    @pl.when(even)
+    def _():
+        for piece in pass_on:
+            piece.wait_send()
+
+    @pl.when(jnp.logical_not(even))
+    def _():
+        lower_out.wait_send()
+        lower_on.wait_send()
+
     for i in range(held):
         @pl.when(slot_of(i) < STEPS)
         def _():
@@ -304,6 +350,9 @@
             dma((STEPS,)),
             dma((STEPS - 1, samples // 128)),
             dma((STEPS - 1, samples // 128)),
+            dma((3,)),
+            dma((1,)),
+            pltpu.VMEM((samples + FLAG_ROWS, cols), jnp.bfloat16),
         ],
         compiler_params=pltpu.CompilerParams(
             collective_id=0, has_side_effects=True, vmem_limit_bytes=20 * 1024 * 1024

time: 20.1 us -> 19.3 us (0.960)
  Pallas kernels: 20 us -> 19.1 us
    pallas_call x1, Pallas kernels: 17.2 us -> 16.3 us  [shards(): pl.pallas_call(functools.partial(gather_kernel, nrow, ncol), out_shape=(j...]
where the time goes in v4:
time: 19.3 us; the launch traced here: 19.2 us
  Pallas kernels  19.1 us (99%)
    pallas_call x1, Pallas kernels, shards(): pl.pallas_call(functools.partial(gather_kernel, nrow, ncol), out_shape=(j...  16.3 us
    pallas_call x1, Pallas kernels, shards(): pl.pallas_call(correlate_kernel, out_shape=jax.ShapeDtypeStruct((lags, co...  2.8 us

profile of v4, /device:TPU:0, one launch (start us, length us, event | category | flops | bytes accessed | tf_op | source)
XLA Modules:
  0.0 19.2 jit_solution(1896101595671080699)
XLA Ops:
  0.0 16.3 %gather.1 = (bf16[1152,416]{1,0:T(8,128)(2,1)S(1)}, bf16[416,1024]{1,0:T(8,128)(2,1)S(1)}, f32[65,128,128]{2,1,0:T(8,128)S(1)}, f32[128,128]{1,0:T(8,128)S(1)}) custom-call(bf16[2,128,384]{2,1,0:T(8,128)(2,1)} %rr.1, s32[2,128]{1,0:T(2,128)} %rv.1, bf16[1,128,384]{2,1,0:T(8,128)(2,1)} %cr.1, s32[1,128]{1,0:T(1,128)} %cv.1), custom_call_target="tpu_custom_call" | custom-call | tf_op jit(solution)/shard_map/gather/pallas_call | solution.py:324
  16.4 2.8 %correlate.1 = f32[65,128,128]{2,1,0:T(8,128)} custom-call(bf16[1152,416]{1,0:T(8,128)(2,1)S(1)} %get-tuple-element.9.stacked, bf16[416,1024]{1,0:T(8,128)(2,1)S(1)} %get-tuple-element.10.weights, f32[65,128,128]{2,1,0:T(8,128)S(1)} %get-tuple-element.11.partial, f32[128,128]{1,0:T(8,128)S(1)} %get-tuple-element.12.scale), custom_call_target="tpu_custom_call" | custom-call | tf_op jit(solution)/shard_map/correlate/pallas_call | solution.py:362

commit v5 on v4

--- a/solution.py
+++ b/solution.py
@@ -84,7 +84,7 @@
     pass_back = right_copy(right.at[1], 1, 1, -1)
     pass_on = right_copy(right.at[1], 3, 2, 1)
 
-    cut = FLAG_ROWS * -(-(samples + FLAG_ROWS) // (2 * FLAG_ROWS))
+    cut = FLAG_ROWS * (5 * (samples + FLAG_ROWS) // (6 * FLAG_ROWS) + 1)
     upper, lower, lower_here = slice(0, cut), slice(cut, samples + FLAG_ROWS), slice(0, samples + FLAG_ROWS - cut)
 
     def relay_copy(source, target, sender, receiver, step):
@@ -204,6 +204,12 @@
         upper_out.wait_recv()
         upper_on.start()
 
+    def pairs(s):
+        source = send_right if s == 0 else right.at[s - 1]
+        col_flag = source[samples : samples + FLAG_ROWS, :].astype(jnp.float32)[0:1, :]
+        row_flag = left[s, samples : samples + FLAG_ROWS, :].astype(jnp.float32)[0:1, :]
+        return jnp.broadcast_to(col_flag, (cols, cols)).T * row_flag
+
     stack(0, send_right)
     left_pass(0)
     left_wait(0)
@@ -239,6 +245,7 @@
     multiply(2 * samples, 3 * samples, True)
     left_wait(3)
     weigh(3, 3)
+    scale[...] = pairs(0) + pairs(1) + pairs(2)
     @pl.when(even)
     def _():
         upper_on.wait_recv()
@@ -249,12 +256,7 @@
         right_wait(3)
 
     stack(3, right.at[2])
-    count = jnp.zeros((cols, rows), jnp.float32)
-    for s in range(STEPS):
-        source = send_right if s == 0 else right.at[s - 1]
-        col_flag = source[samples : samples + FLAG_ROWS, :].astype(jnp.float32)[0:1, :]
-        row_flag = left[s, samples : samples + FLAG_ROWS, :].astype(jnp.float32)[0:1, :]
-        count = count + jnp.broadcast_to(col_flag, (cols, cols)).T * row_flag
+    count = scale[...] + pairs(3)
     scale[...] = 1.0 / (jnp.sqrt(jnp.float32(samples)) * jnp.maximum(count, 1.0))
 
     for piece in two_on + own_on:

time: 19.3 us -> 19 us (0.984)
  Pallas kernels: 19.1 us -> 18.8 us
    pallas_call x1, Pallas kernels: 16.3 us -> 16 us  [shards(): pl.pallas_call(functools.partial(gather_kernel, nrow, ncol), out_shape=(j...]
where the time goes in v5:
time: 19 us; the launch traced here: 18.8 us
  Pallas kernels  18.8 us (99%)
    pallas_call x1, Pallas kernels, shards(): pl.pallas_call(functools.partial(gather_kernel, nrow, ncol), out_shape=(j...  16 us
    pallas_call x1, Pallas kernels, shards(): pl.pallas_call(correlate_kernel, out_shape=jax.ShapeDtypeStruct((lags, co...  2.8 us

profile of v5, /device:TPU:0, one launch (start us, length us, event | category | flops | bytes accessed | tf_op | source)
XLA Modules:
  0.0 18.8 jit_solution(5849640202364192410)
XLA Ops:
  0.0 16.0 %gather.1 = (bf16[1152,416]{1,0:T(8,128)(2,1)S(1)}, bf16[416,1024]{1,0:T(8,128)(2,1)S(1)}, f32[65,128,128]{2,1,0:T(8,128)S(1)}, f32[128,128]{1,0:T(8,128)S(1)}) custom-call(bf16[2,128,384]{2,1,0:T(8,128)(2,1)} %rr.1, s32[2,128]{1,0:T(2,128)} %rv.1, bf16[1,128,384]{2,1,0:T(8,128)(2,1)} %cr.1, s32[1,128]{1,0:T(1,128)} %cv.1), custom_call_target="tpu_custom_call" | custom-call | tf_op jit(solution)/shard_map/gather/pallas_call | solution.py:326
  16.0 2.8 %correlate.1 = f32[65,128,128]{2,1,0:T(8,128)} custom-call(bf16[1152,416]{1,0:T(8,128)(2,1)S(1)} %get-tuple-element.9.stacked, bf16[416,1024]{1,0:T(8,128)(2,1)S(1)} %get-tuple-element.10.weights, f32[65,128,128]{2,1,0:T(8,128)S(1)} %get-tuple-element.11.partial, f32[128,128]{1,0:T(8,128)S(1)} %get-tuple-element.12.scale), custom_call_target="tpu_custom_call" | custom-call | tf_op jit(solution)/shard_map/correlate/pallas_call | solution.py:364
